TPU v7x, 32 devices: a whole 2x2x4 slice. The times are simulated.
32 devices in a mesh: req: 32 (over z, y, x, core), mlp: 1.
Axes of the slice: x: 2, y: 2, z: 4, core: 2. Of those that a mesh axis runs over, the one named last changes fastest.
Arguments:
- queries: bfloat16 [8192, 8, 256], P('req', 'mlp'), may hold values from -7 to 7
- new_kv: bfloat16 [8192, 8, 512], P('req', 'mlp'), may hold values from -6 to 6
- cache_pool: bfloat16 [192, 128, 8, 512], P('req', None, 'mlp'), may hold values from -6 to 6
- page_table: int32 [32, 6], P('req'), may hold values from 0 to 5, each once within a row
- assignment: int32 [32], P('req'), may hold values from 0 to 31, each once
- lengths: int32 [32], replicated, may hold values from 1 to 768, 6144 in all
- lambda_vectors: float32 [4, 128], replicated, may hold values from -0.4 to 0.4
- subln_gain: float32 [256], replicated, may hold values from 0.5 to 1.5
- residual: bfloat16 [8192, 2048], P('req', 'mlp'), may hold values from -70 to 70
- out_weight: bfloat16 [2048, 2048], P('req', 'mlp'), may hold values from -0.125 to 0.125
- norm_gain: float32 [2048], replicated, may hold values from 0.5 to 1.5
- gate_weight: bfloat16 [2048, 3072], P('req', 'mlp'), may hold values from -0.125 to 0.125
- up_weight: bfloat16 [2048, 3072], P('req', 'mlp'), may hold values from -0.125 to 0.125
- down_weight_t: bfloat16 [2048, 3072], P('req', 'mlp'), may hold values from -0.109375 to 0.109375
Outputs:
- layer_out: bfloat16 [8192, 2048], P('req', 'mlp')
Inputs may be any that keep to these rules, and one draw needn't show every extreme that they name: `page_table`: row g lists the cache pages of slot g in logical order as offsets from page g * 6; each offset once in a row. `assignment`: every request is served by exactly one slot. `lengths`: indexed by request; some request has exactly 768 cached tokens.
All inputs are finite; a program needn't handle non-finite values.
Results may differ from a plain program's by a relative error of at most 0.011.
Values may be sent and summed in bfloat16 or wider, within the bound.
A program may use at most 128 MiB of HBM per device.

v0:
```python
import jax
import jax.numpy as jnp
from jax import lax
from jax.sharding import PartitionSpec as P

D = 2048


NEG_FILL = -1e30
LAMBDA_BASE = 0.2


def map_block(carried, query_rows, key_half, value_rows, visible, score_scale):
    running_max, running_sum, running_acc = carried
    score = (
        jnp.einsum("nhd,khd->nhk", query_rows, key_half, preferred_element_type=jnp.float32)
        * score_scale
    )
    score = jnp.where(visible[:, None, :], score, NEG_FILL)
    newest = jnp.maximum(running_max, jnp.max(score, axis=2))
    exp_terms = jnp.where(visible[:, None, :], jnp.exp(score - newest[:, :, None]), 0.0)
    shrink = jnp.exp(running_max - newest)
    running_sum = running_sum * shrink + jnp.sum(exp_terms, axis=2)
    running_acc = running_acc * shrink[:, :, None] + jnp.einsum(
        "nhk,khd->nhd",
        exp_terms.astype(jnp.bfloat16),
        value_rows,
        preferred_element_type=jnp.float32,
    )
    return (newest, running_sum, running_acc)


def both_maps(carried, query_rows, key_rows, visible, half_size):
    score_scale = half_size ** (-0.5)
    value_rows = key_rows[:, :, 2 * half_size :]
    map_one = map_block(
        carried[0],
        query_rows[:, :, :half_size],
        key_rows[:, :, :half_size],
        value_rows,
        visible,
        score_scale,
    )
    map_two = map_block(
        carried[1],
        query_rows[:, :, half_size:],
        key_rows[:, :, half_size : 2 * half_size],
        value_rows,
        visible,
        score_scale,
    )
    return (map_one, map_two)


def attend(
    queries, new_kv, cache_pool, page_table, assignment, lengths, lambda_vectors, subln_gain
):
    row_count, head_count, value_width = queries.shape
    half_size = value_width // 2
    page_len = cache_pool.shape[1]
    request = assignment[0]
    cached = jnp.sum(
        jnp.where(jnp.arange(lengths.shape[0], dtype=jnp.int32) == request, lengths, 0)
    )

    def fresh_state():
        return (
            jnp.full((row_count, head_count), NEG_FILL, jnp.float32),
            jnp.zeros((row_count, head_count), jnp.float32),
            jnp.zeros((row_count, head_count, value_width), jnp.float32),
        )

    table_row = page_table[0]

    def page_step(page_index, carried):
        physical = table_row[page_index]
        page_rows = lax.dynamic_index_in_dim(cache_pool, physical, 0, keepdims=False)
        positions = page_index * page_len + jnp.arange(page_len, dtype=jnp.int32)
        visible = jnp.broadcast_to((positions < cached)[None, :], (row_count, page_len))
        return both_maps(carried, queries, page_rows, visible, half_size)

    page_count = (cached + page_len - 1) // page_len
    carried = lax.fori_loop(jnp.int32(0), page_count, page_step, (fresh_state(), fresh_state()))
    token_pos = jnp.arange(row_count, dtype=jnp.int32)
    carried = both_maps(
        carried, queries, new_kv, token_pos[None, :] <= token_pos[:, None], half_size
    )
    lambda_now = (
        jnp.exp(jnp.sum(lambda_vectors[0] * lambda_vectors[1]))
        - jnp.exp(jnp.sum(lambda_vectors[2] * lambda_vectors[3]))
        + LAMBDA_BASE
    )
    mix_out = (
        carried[0][2] / carried[0][1][:, :, None]
        - lambda_now * carried[1][2] / carried[1][1][:, :, None]
    )
    mix_out = (
        mix_out
        * lax.rsqrt(jnp.mean(mix_out * mix_out, axis=2, keepdims=True) + 1e-05)
        * subln_gain
        * (1.0 - LAMBDA_BASE)
    )
    return mix_out.astype(jnp.bfloat16).reshape(row_count, head_count * value_width)


def per_device(
    queries,
    new_kv,
    cache_pool,
    page_table,
    assignment,
    lengths,
    lambda_vectors,
    subln_gain,
    residual,
    out_weight,
    norm_gain,
    gate_weight,
    up_weight,
    down_weight_t,
):
    attn_out = attend(
        queries, new_kv, cache_pool, page_table, assignment, lengths, lambda_vectors, subln_gain
    )
    heads_all = lax.all_gather(attn_out, "mlp", axis=1, tiled=True)
    columns = heads_all
    projected = jnp.dot(
        columns,
        lax.all_gather(out_weight, "req", axis=0, tiled=True),
        preferred_element_type=jnp.float32,
    )
    stream = (residual.astype(jnp.float32) + projected).astype(jnp.bfloat16)
    stream_f = stream.astype(jnp.float32)
    squares = lax.psum(jnp.sum(stream_f * stream_f, axis=1), "mlp")
    slice_width = stream_f.shape[1]
    local_gain = lax.dynamic_slice_in_dim(
        norm_gain, lax.axis_index("mlp") * slice_width, slice_width
    )
    normed_part = (stream_f * lax.rsqrt(squares / D + 1e-05)[:, None] * local_gain).astype(
        jnp.bfloat16
    )
    normed = lax.all_gather(normed_part, "mlp", axis=1, tiled=True)
    columns = normed
    gate_value = jnp.dot(
        columns,
        lax.all_gather(gate_weight, "req", axis=0, tiled=True),
        preferred_element_type=jnp.float32,
    )
    up_value = jnp.dot(
        columns,
        lax.all_gather(up_weight, "req", axis=0, tiled=True),
        preferred_element_type=jnp.float32,
    )
    hidden_act = (jax.nn.silu(gate_value) * up_value).astype(jnp.bfloat16)
    partial_value = lax.dot_general(
        hidden_act,
        lax.all_gather(down_weight_t, "req", axis=0, tiled=True),
        (((1,), (1,)), ((), ())),
        preferred_element_type=jnp.float32,
    )
    summed = lax.psum_scatter(
        partial_value.astype(jnp.bfloat16), "mlp", scatter_dimension=1, tiled=True
    ).astype(jnp.float32)
    return (stream_f + summed).astype(jnp.bfloat16)


def solution(mesh):
    in_specs = (
        P("req", "mlp", None),
        P("req", "mlp", None),
        P("req", None, "mlp", None),
        P("req", None),
        P("req"),
        P(),
        P(),
        P(),
        P("req", "mlp"),
        P("req", "mlp"),
        P(),
        P("req", "mlp"),
        P("req", "mlp"),
        P("req", "mlp"),
    )
    out_specs = P("req", "mlp")
    return jax.shard_map(
        per_device, mesh=mesh, in_specs=in_specs, out_specs=out_specs, check_vma=False
    )
```

profile of v0, /device:TPU:0, one launch (start us, length us, event | category | flops | bytes accessed | tf_op | source)
XLA Modules:
  0.0 402.2 jit_solution(6046080303822611643)
XLA Ops:
  6.5 0.7 all-gather.5.cloned.1.call-update
  7.3 0.7 all-gather.7.cloned.1.call-update
  8.0 0.0 all-gather.11.cloned.1.call-start
  8.1 0.7 all-gather.11.cloned.1.call-update
  8.8 0.5 all-gather.9.cloned.1.call-update
  10.0 1.3 fusion.64
  11.9 1.2 copy.20
  13.1 0.2 slice-done
  13.4 1.6 copy.36
  15.0 0.6 multiply_reduce_fusion.1
  17.0 0.9 fusion.74
  17.9 1.8 fusion.35
  19.7 0.2 broadcast.72
  19.9 1.5 broadcast.72.clone
  21.4 21.3 %while.20 = (s32[]{:T(128)}, f32[256,8]{0,1:T(8,128)S(1)}, f32[256,8]{0,1:T(8,128)S(1)}, f32[256,8,256]{0,2,1:T(8,128)S(1)}, f32[256,8]{0,1:T(8,128)S(1)}, /*ind...) while((s32[]{:T(128)}, f32[256,8]{0,1:T(8,128)S(1)}, ...), condition=%wide.region_6.7_spmd, body=%wide.region_1.6_spmd.sunk | while | flops 409477376 | bytes 38537780 | solution.py:83
  21.4 0.7 dynamic_slice.12
  24.1 1.3 constant_dynamic-slice_fusion.2
  25.4 0.3 copy.49
  25.8 0.6 add_compare_fusion.2
  26.4 1.4 fusion.93
  27.8 1.5 fusion.94
  29.3 0.4 fusion.95
  29.8 1.0 bitcast_add_fusion.7
  30.7 1.0 bitcast_add_fusion.6
  31.7 0.3 copy-done.1
  32.0 0.7 dynamic_slice.12
  34.7 1.3 constant_dynamic-slice_fusion.2
  36.0 0.3 copy.49
  36.4 0.6 add_compare_fusion.2
  37.0 1.4 fusion.93
  38.4 1.5 fusion.94
  39.9 0.4 fusion.95
  40.4 1.0 bitcast_add_fusion.7
  41.4 1.0 bitcast_add_fusion.6
  42.3 0.3 copy-done.1
  42.7 4.2 %fusion.37 = (f32[256,8]{0,1:T(8,128)S(1)}, f32[256,8]{0,1:T(8,128)S(1)}, f32[8,256,256]{2,1,0:T(8,128)}) fusion(f32[8,256,256]{2,1,0:T(8,128)} %get-tuple-element.138, f32[256,8]{0,1:T(8,128)S(1)} %max.12, pred[256,256]{0,1:T(8,128)(4,1)S(1)} %iota_compare_fusion, bf16[256,8,256]{2,0,1:T(8,128)(2,1)} %get-tuple-element.293, ...), kind=kOutput, calls=%fused_computation.62 | convolution fusion | flops 138407936 | bytes 5332992 | tf_op jit(solution)/shard_map/nhd,khd->nhk/dot_general | solution.py:16
  46.9 2.2 fusion.39
  49.2 2.5 fusion.42
  51.7 0.4 copy-done.5
  52.0 1.4 multiply_reduce_fusion
  53.5 0.3 multiply_convert_fusion
  53.8 36.6 %all-gather.5.cloned.1.call-done = bf16[2048,2048]{1,0:T(8,128)(2,1)} async-done(((bf16[64,2048]{1,0:T(8,128)(2,1)}), bf16[2048,2048]{1,0:T(8,128)(2,1)}) %all-gather.5.cloned.1.call-update) | async-done | bytes 8388624 | tf_op jit(solution)/shard_map/all_gather | solution.py:129
  90.4 5.9 %fusion.28 = (f32[256]{0:T(256)S(1)}, bf16[256,2048]{1,0:T(8,128)(2,1)S(1)}) fusion(bf16[256,2048]{0,1:T(8,128)(2,1)S(1)} %bitcast.73, bf16[2048,2048]{1,0:T(8,128)(2,1)} %all-gather.5.cloned.1.call-done, bf16[256,2048]{1,0:T(8,128)(2,1)S(1)} %copy-done.6), kind=kOutput, calls=%fused_computation.45 | convolution fusion | flops 2150629120 | bytes 11535360 | tf_op jit(solution)/shard_map/dot_general | solution.py:127
  96.3 91.5 %all-gather.7.cloned.1.call-done = bf16[2048,3072]{1,0:T(8,128)(2,1)} async-done(((bf16[64,3072]{1,0:T(8,128)(2,1)}), bf16[2048,3072]{1,0:T(8,128)(2,1)}) %all-gather.7.cloned.1.call-update) | async-done | bytes 12582928 | tf_op jit(solution)/shard_map/all_gather | solution.py:146
  187.8 9.8 %fusion.62 = f32[256,3072]{1,0:T(8,128)} fusion(bf16[2048,3072]{1,0:T(8,128)(2,1)} %all-gather.7.cloned.1.call-done, bf16[256,2048]{1,0:T(8,128)(2,1)S(1)} %get-tuple-element.143, f32[2048]{0:T(1024)S(1)} %copy-done.11, f32[256]{0:T(256)S(1)} %add_rsqrt_fusion.1), kind=kOutput, calls=%fused_computation.83 | convolution fusion | flops 3223322624 | bytes 16786432 | tf_op jit(solution)/shard_map/dot_general | solution.py:144
  197.6 87.4 %all-gather.11.cloned.1.call-done = bf16[2048,3072]{1,0:T(8,128)(2,1)} async-done(((bf16[64,3072]{1,0:T(8,128)(2,1)}), bf16[2048,3072]{1,0:T(8,128)(2,1)}) %all-gather.11.cloned.1.call-update) | async-done | bytes 12582928 | tf_op jit(solution)/shard_map/all_gather | solution.py:157
  284.9 97.0 %all-gather.9.cloned.1.call-done = bf16[2048,3072]{1,0:T(8,128)(2,1)} async-done(((bf16[64,3072]{1,0:T(8,128)(2,1)}), bf16[2048,3072]{1,0:T(8,128)(2,1)}) %all-gather.9.cloned.1.call-update) | async-done | bytes 12582928 | tf_op jit(solution)/shard_map/all_gather | solution.py:151
  381.9 13.8 %fusion.27 = bf16[256,2048]{1,0:T(8,128)(2,1)} fusion(bf16[2048,3072]{1,0:T(8,128)(2,1)} %all-gather.11.cloned.1.call-done, bf16[256,2048]{1,0:T(8,128)(2,1)S(1)} %get-tuple-element.143, bf16[2048,3072]{1,0:T(8,128)(2,1)} %all-gather.9.cloned.1.call-done, f32[256,3072]{1,0:T(8,128)} %fusion.62, f32[2048]{0:T(1024)S(1)} %copy-done.11, ...), kind=kOutput, calls=%fused_computation.44 | convolution fusion | flops 6451888128 | bytes 30417920 | tf_op jit(solution)/shard_map/dot_general | solution.py:155
  (51 shorter events, 0.3 us)
Async XLA Ops:
  6.5 5.4 %copy-start.7 = (bf16[256,8,256]{2,1,0:T(8,128)(2,1)S(1)}, bf16[256,8,256]{2,1,0:T(8,128)(2,1)}, u32[]{:S(2)}) copy-start(bf16[256,8,256]{2,1,0:T(8,128)(2,1)} %param.16) | copy-start | bytes 3145732
  6.5 83.9 %all-gather.5.cloned.1.call-start = ((), (), s32[]{:S(2)}) async-start(), calls=%async_computation | async-start | bytes 8650752 | tf_op jit(solution)/shard_map/all_gather | solution.py:129
  7.3 180.5 %all-gather.7.cloned.1.call-start = ((), (), s32[]{:S(2)}) async-start(), calls=%async_computation.1 | async-start | bytes 12976128 | tf_op jit(solution)/shard_map/all_gather | solution.py:146
  8.0 276.9 %all-gather.11.cloned.1.call-start = ((), (), s32[]{:S(2)}) async-start(), calls=%async_computation.3 | async-start | bytes 12976128 | tf_op jit(solution)/shard_map/all_gather | solution.py:157
  8.7 373.2 %all-gather.9.cloned.1.call-start = ((), (), s32[]{:S(2)}) async-start(), calls=%async_computation.2 | async-start | bytes 12976128 | tf_op jit(solution)/shard_map/all_gather | solution.py:151
  11.9 1.4 slice-start
  13.1 1.9 copy-start.9
  13.1 3.9 copy-start.3
  15.0 2.9 copy-start.8
  19.7 1.7 copy-start.12
  27.8 2.0 copy-start
  30.7 1.3 copy-start.1
  38.4 2.0 copy-start
  41.4 1.3 copy-start.1
  46.9 2.2 copy-start.4
  49.1 2.5 copy-start.2
  49.1 2.9 copy-start.5
  52.0 1.4 copy-start.10
  53.4 37.0 %copy-start.6 = (bf16[256,2048]{1,0:T(8,128)(2,1)S(1)}, bf16[256,2048]{1,0:T(8,128)(2,1)}, u32[]{:S(2)}) copy-start(bf16[256,2048]{1,0:T(8,128)(2,1)} %param.24) | copy-start | bytes 3145732
  90.4 97.4 %copy-start.11 = (f32[2048]{0:T(1024)S(1)}, f32[2048]{0:T(1024)}, u32[]{:S(2)}) copy-start(f32[2048]{0:T(1024)} %param.26) | copy-start | bytes 24580
Sparse Core Ops, SparseCore 0:
  10.2 80.1 all-gather.4
  93.3 94.4 all-gather.6
  190.7 94.2 all-gather.10
  287.6 94.2 all-gather.8
where the time goes:
time: 403 us; the launch traced here: 402 us
  waiting for transfers between devices  315 us (78%)
  matrix products  48.9 us (12%)
  between operations  15.9 us (4%)
  local copies, waits for them, and re-layouts  11.2 us (3%)
  other arithmetic  6.6 us (2%)
  loops' own time  4.33 us (1%)
    all_gather x1, waiting for transfers between devices, per_device(): lax.all_gather(up_weight, 'req', axis=0, tiled=True)  97 us
    all_gather x1, waiting for transfers between devices, per_device(): lax.all_gather(gate_weight, 'req', axis=0, tiled=True)  91.5 us
    all_gather x1, waiting for transfers between devices, per_device(): lax.all_gather(down_weight_t, 'req', axis=0, tiled=True)  87.4 us
    all_gather x1, waiting for transfers between devices, per_device(): lax.all_gather(out_weight, 'req', axis=0, tiled=True)  36.6 us
    dot_general x1, matrix products, per_device(): lax.dot_general(hidden_act, lax.all_gather(down_weight_t, 'req', axis=0,...  13.8 us
    dot_general x6, matrix products, map_block(): jnp.einsum('nhd,khd->nhk', query_rows, key_half, preferred_element_type=j...  11.8 us
    dot_general x1, matrix products, per_device(): jnp.dot(columns, lax.all_gather(gate_weight, 'req', axis=0, tiled=True),...  9.75 us
  transfers between devices with their start and end apart: 4, of which 4 were waited for; matrix products, arithmetic and copies ran while one was open for 13% of the time, Pallas kernels for 0%

commit v1 on v0

--- a/solution.py
+++ b/solution.py
@@ -1,6 +1,8 @@
 import jax
 import jax.numpy as jnp
 from jax import lax
+from jax.experimental import pallas as pl
+from jax.experimental.pallas import tpu as pltpu
 from jax.sharding import PartitionSpec as P
 
 D = 2048
@@ -164,6 +166,507 @@
     return (stream_f + summed).astype(jnp.bfloat16)
 
 
+BF16, F32 = jnp.bfloat16, jnp.float32
+MESH = pl.DeviceIdType.MESH
+
+
+def layer_kernel(
+    scale_ref, bias_ref, gain_ref, norm_ref, residual_ref,
+    q_hbm, kv_hbm, out_hbm, gate_hbm, up_hbm, down_hbm,
+    result_ref,
+    q_buf, kv_buf, attn, wo, wg, wu, wd, normed, stream, hidden, part, got_core, to_x, got_x,
+    load_sem, own_sem, first_send, first_recv, far_send, far_recv, o_send, o_recv,
+    n_send, n_recv, d_send, d_recv,
+):
+    heads = q_buf.shape[0]
+    rows = q_buf.shape[1]
+    wide = q_buf.shape[2]
+    half = wide // 2
+    width = stream.shape[1]
+    units = wg.shape[2]
+    shard = out_hbm.shape[0]
+    halfw = width // 2
+
+    me = lax.axis_index("req")
+    core = me % 2
+    x = (me // 2) % 2
+    quarter = me % 4
+    y = (me // 4) % 2
+    z = me // 8
+    base = me - quarter
+    side = z // 2
+    inner = z + side * (3 - 2 * z)
+    q_core = quarter + 1 - 2 * core
+    q_x = (quarter + 2) % 4
+    q_diag = (q_core + 2) % 4
+    at_core, at_x, at_diag = base + q_core, base + q_x, base + q_diag
+    at_y = me + 4 - 8 * y
+    off = me - 8 * z
+    at_n = off + 8 * (1 + side)
+    at_e = off + 8 * (3 * side)
+    at_m = off + 8 * (2 - side)
+    is_end = inner == 0
+    is_mid = inner == 1
+
+    def order(k):
+        o = k + inner * (1 - 2 * k) * (1 - k // 2)
+        return o + side * (3 - 2 * o)
+
+    def send(src, dst, ssem, rsem, device):
+        return pltpu.make_async_remote_copy(
+            src_ref=src, dst_ref=dst, send_sem=ssem, recv_sem=rsem,
+            device_id={"req": device}, device_id_type=MESH,
+        )
+
+    barrier = pltpu.get_barrier_semaphore()
+
+    def greet(device):
+        pl.semaphore_signal(barrier, inc=1, device_id={"req": device}, device_id_type=MESH)
+
+    for device in (at_core, at_x, at_diag, at_y):
+        greet(device)
+
+    @pl.when(is_end)
+    def _():
+        greet(at_n)
+        pl.semaphore_wait(barrier, 5)
+
+    @pl.when(is_mid)
+    def _():
+        greet(at_e)
+        greet(at_m)
+        pl.semaphore_wait(barrier, 6)
+
+    my_half = pl.ds(pl.multiple_of(core * halfw, 128), halfw)
+    other_half = pl.ds(pl.multiple_of((1 - core) * halfw, 128), halfw)
+    my_rows = pl.ds(pl.multiple_of(quarter * shard, 64), shard)
+    core_rows = pl.ds(pl.multiple_of(q_core * shard, 64), shard)
+    x_rows = pl.ds(pl.multiple_of(x * 2 * shard, 128), 2 * shard)
+    other_x_rows = pl.ds(pl.multiple_of((1 - x) * 2 * shard, 128), 2 * shard)
+
+    o_own = pltpu.make_async_copy(out_hbm.at[:, my_half], wo.at[z, y, my_rows, my_half], own_sem.at[0])
+    o_own.start()
+    o_core = send(
+        out_hbm.at[:, other_half], wo.at[z, y, my_rows, other_half], o_send.at[0], o_recv.at[0], at_core
+    )
+    o_core.start()
+
+    firsts = []
+    owns = []
+    for m, (src, dst) in enumerate(((gate_hbm, wg), (up_hbm, wu), (down_hbm, wd))):
+        block = dst.at[z * 2 + y, my_rows]
+        mine = pltpu.make_async_copy(
+            src.at[:, pl.ds(pl.multiple_of(quarter * units, 128), units)], block, own_sem.at[1 + m]
+        )
+        mine.start()
+        owns.append(mine)
+        group = []
+        for k, (q_to, device) in enumerate(((q_core, at_core), (q_x, at_x), (q_diag, at_diag))):
+            copy = send(
+                src.at[:, pl.ds(pl.multiple_of(q_to * units, 128), units)],
+                block, first_send.at[m, k], first_recv.at[m, k], device,
+            )
+            copy.start()
+            group.append(copy)
+        firsts.append(group)
+
+    def load(h):
+        return (
+            pltpu.make_async_copy(q_hbm.at[h], q_buf.at[h], load_sem.at[0, h]),
+            pltpu.make_async_copy(kv_hbm.at[h], kv_buf.at[h], load_sem.at[1, h]),
+        )
+
+    def start_load(h, carry):
+        for copy in load(h):
+            copy.start()
+        return carry
+
+    lax.fori_loop(0, heads, start_load, 0)
+
+    mats = (wg, wu, wd)
+
+    def along_z(block_at, send_sems, recv_sems, k):
+        block = block_at(order(k))
+
+        def to_end(slot):
+            return send(block, block, send_sems(slot), recv_sems(slot), at_e)
+
+        def to_mid(slot, at):
+            return send(block, block, send_sems(at), recv_sems(slot), at_m)
+
+        if k == 0:
+            return (
+                [send(block, block, send_sems(1), recv_sems(1), at_n)],
+                [to_end(1), to_mid(2, 4)],
+            )
+        if k == 1:
+            return [], [to_mid(3, 5)]
+        return [], [to_end(k)]
+
+    def z_start(copies):
+        for_end, for_mid = copies
+        if for_end:
+            @pl.when(is_end)
+            def _():
+                for copy in for_end:
+                    copy.start()
+
+        @pl.when(is_mid)
+        def _():
+            for copy in for_mid:
+                copy.start()
+
+    def z_wait_send(copies):
+        for_end, for_mid = copies
+        if for_end:
+            @pl.when(is_end)
+            def _():
+                for copy in for_end:
+                    copy.wait_send()
+
+        @pl.when(is_mid)
+        def _():
+            for copy in for_mid:
+                copy.wait_send()
+
+    def f_block(m):
+        return lambda zz: mats[m].at[zz * 2 + y]
+
+    def f_z(m, k):
+        return along_z(
+            f_block(m), lambda i: far_send.at[m, i], lambda i: far_recv.at[m, i], k
+        )
+
+    def f_z_recv(m, k):
+        block = f_block(m)(order(k))
+        send(block, block, far_send.at[m, k], far_recv.at[m, k], at_y).wait_recv()
+
+    def f_y(m, k):
+        block = f_block(m)(order(k))
+        return send(block, block, far_send.at[m, 6 + k], far_recv.at[m, 6 + k], at_y)
+
+    def f_y_recv(m, k):
+        block = mats[m].at[order(k) * 2 + 1 - y]
+        send(block, block, far_send.at[m, 6 + k], far_recv.at[m, 6 + k], at_y).wait_recv()
+
+    def f_first(m):
+        owns[m].wait()
+        for i, q_from in enumerate((q_core, q_x, q_diag)):
+            block = mats[m].at[z * 2 + y, pl.ds(pl.multiple_of(q_from * shard, 64), shard)]
+            send(block, block, first_send.at[m, i], first_recv.at[m, i], at_core).wait_recv()
+        f_y(m, 0).start()
+
+    def f_pass(m, k):
+        f_z_recv(m, k)
+        z_start(f_z(m, k))
+        f_y(m, k).start()
+
+    def o_block(zz):
+        return wo.at[zz, :, x_rows, my_half]
+
+    def o_z(k):
+        return along_z(o_block, lambda i: o_send.at[1 + i], lambda i: o_recv.at[1 + i], k)
+
+    def o_x(k):
+        block = o_block(order(k))
+        return send(block, block, o_send.at[8 + k], o_recv.at[8 + k], at_x)
+
+    def o_c(k):
+        block = wo.at[order(k), :, :, my_half]
+        return send(block, block, o_send.at[12 + k], o_recv.at[12 + k], at_core)
+
+    def o_y():
+        block = wo.at[z, y, x_rows, my_half]
+        return send(block, block, o_send.at[1], o_recv.at[1], at_y)
+
+    def o_first():
+        o_own.wait()
+        block = wo.at[z, y, core_rows, my_half]
+        send(block, block, o_send.at[0], o_recv.at[0], at_core).wait_recv()
+        o_y().start()
+
+    def o_second():
+        block = wo.at[z, 1 - y, x_rows, my_half]
+        send(block, block, o_send.at[1], o_recv.at[1], at_y).wait_recv()
+        z_start(o_z(0))
+        o_x(0).start()
+
+    def o_pass(k):
+        block = o_block(order(k))
+        send(block, block, o_send.at[1 + k], o_recv.at[1 + k], at_y).wait_recv()
+        z_start(o_z(k))
+        o_x(k).start()
+
+    def o_share(k):
+        block = wo.at[order(k), :, other_x_rows, my_half]
+        send(block, block, o_send.at[8 + k], o_recv.at[8 + k], at_x).wait_recv()
+        o_c(k).start()
+
+    def o_shared(k):
+        block = wo.at[order(k), :, :, other_half]
+        send(block, block, o_send.at[12 + k], o_recv.at[12 + k], at_core).wait_recv()
+
+    def z_open(m):
+        z_start(f_z(m, 0))
+
+    o_first()
+    f_first(0)
+    o_second()
+
+    events = {
+        0: lambda: f_first(1),
+        1: lambda: (z_open(0), o_pass(1), o_share(0)),
+        2: lambda: f_first(2),
+        3: lambda: (o_pass(2), z_open(1)),
+        4: lambda: (o_share(1), f_pass(0, 1)),
+        5: lambda: (o_pass(3), o_share(2)),
+        6: lambda: (f_pass(0, 2), z_open(2)),
+        7: lambda: (f_pass(1, 1), f_pass(0, 3)),
+    }
+
+    lam = scale_ref[0]
+    bias = bias_ref[...]
+    causal = jnp.where(
+        lax.broadcasted_iota(jnp.int32, (rows, rows), 1)
+        <= lax.broadcasted_iota(jnp.int32, (rows, rows), 0),
+        0.0,
+        NEG_FILL,
+    ).astype(F32)
+
+    def head_step(h, carry):
+        for copy in load(h):
+            copy.wait()
+        values = kv_buf[h, :, wide:]
+        mixed = []
+        for one in range(2):
+            lanes = slice(one * half, (one + 1) * half)
+            score = lax.dot_general(
+                q_buf[h, :, lanes], kv_buf[h, :, lanes], (((1,), (1,)), ((), ())),
+                preferred_element_type=F32,
+            ) * (half ** -0.5)
+            cached = bias.shape[1]
+            score = jnp.concatenate(
+                [score[:, :cached] + bias, score[:, cached:] + causal], axis=1
+            )
+            expo = jnp.exp(score - jnp.max(score, axis=1, keepdims=True))
+            total = jnp.sum(expo, axis=1, keepdims=True)
+            mixed.append(jnp.dot(expo.astype(BF16), values, preferred_element_type=F32) / total)
+        mix = mixed[0] - lam * mixed[1]
+        mix = mix * lax.rsqrt(jnp.mean(mix * mix, axis=1, keepdims=True) + 1e-05)
+        mix = mix * gain_ref[...] * (1.0 - LAMBDA_BASE)
+        attn[:, pl.ds(pl.multiple_of(h * wide, 128), wide)] = mix.astype(BF16)
+        for i, event in events.items():
+            @pl.when(h == i)
+            def _(event=event):
+                event()
+        return carry
+
+    lax.fori_loop(0, heads, head_step, 0)
+
+    o_share(3)
+    f_pass(1, 2)
+    f_pass(1, 3)
+    for k in range(4):
+        o_shared(k)
+
+    tile = 2 * half
+
+    def project(n, carry):
+        lanes = pl.ds(pl.multiple_of(n * tile, 128), tile)
+        weight = wo[:, :, :, lanes].reshape(width, tile)
+        value = jnp.dot(attn[...], weight, preferred_element_type=F32)
+        stream[:, lanes] = (residual_ref[:, lanes].astype(F32) + value).astype(BF16)
+        return carry
+
+    lax.fori_loop(0, width // tile, project, 0)
+    stream_f = stream[...].astype(F32)
+    squares = jnp.mean(stream_f * stream_f, axis=1, keepdims=True)
+    normed[quarter] = (stream_f * lax.rsqrt(squares + 1e-05) * norm_ref[...]).astype(BF16)
+
+    def n_copy(q_from, i, device):
+        block = normed.at[q_from]
+        return send(block, block, n_send.at[i], n_recv.at[i], device)
+
+    n_copy(quarter, 0, at_x).start()
+    n_copy(quarter, 1, at_core).start()
+    f_pass(2, 1)
+    for m in range(2):
+        for k in range(4):
+            f_y_recv(m, k)
+
+    def feed(i, carry):
+        @pl.when(i == 1)
+        def _():
+            n_copy(q_core, 1, at_core).wait_recv()
+            f_pass(2, 2)
+
+        @pl.when(i == 2)
+        def _():
+            n_copy(q_x, 0, at_x).wait_recv()
+            n_copy(q_x, 2, at_core).start()
+            f_pass(2, 3)
+
+        @pl.when(i == 3)
+        def _():
+            n_copy(q_diag, 2, at_core).wait_recv()
+
+        slot = base_slot(i)
+        tokens = normed[slot]
+
+        def hidden_tile(n, inner_carry):
+            lanes = pl.ds(pl.multiple_of(n * tile, 128), tile)
+            gate = jnp.dot(tokens, wg[:, :, lanes].reshape(width, tile), preferred_element_type=F32)
+            up = jnp.dot(tokens, wu[:, :, lanes].reshape(width, tile), preferred_element_type=F32)
+            hidden[slot, :, lanes] = (gate / (1.0 + jnp.exp(-gate)) * up).astype(BF16)
+            return inner_carry
+
+        lax.fori_loop(0, units // tile, hidden_tile, 0)
+        return carry
+
+    def base_slot(i):
+        q = (quarter + 2 * (i // 2)) % 4
+        flip = i % 2
+        return q + flip * (1 - 2 * (q % 2))
+
+    lax.fori_loop(0, 4, feed, 0)
+
+    def place(j):
+        return order(j // 2) * 2 + (y + j) % 2
+
+    def d_copy(i, p):
+        if i == 0:
+            return send(part.at[q_diag, p], got_core.at[0, p], d_send.at[0, p], d_recv.at[0, p], at_core)
+        if i == 1:
+            return send(part.at[q_core, p], got_core.at[1, p], d_send.at[1, p], d_recv.at[1, p], at_core)
+        return send(to_x.at[p], got_x.at[p], d_send.at[2, p], d_recv.at[2, p], at_x)
+
+    def d_sum(j):
+        p = place(j)
+        d_copy(0, p).wait_recv()
+        to_x[p] = (part[q_x, p].astype(F32) + got_core[0, p].astype(F32)).astype(BF16)
+        d_copy(2, p).start()
+
+    def d_done(j):
+        p = place(j)
+        d_copy(1, p).wait_recv()
+        d_copy(2, p).wait_recv()
+        lanes = pl.ds(pl.multiple_of(p * rows, 128), rows)
+        total = part[quarter, p].astype(F32) + got_core[1, p].astype(F32) + got_x[p].astype(F32)
+        result_ref[:, lanes] = (stream[:, lanes].astype(F32) + total).astype(BF16)
+
+    def down(j, carry):
+        p = place(j)
+
+        @pl.when(j % 2 == 1)
+        def _():
+            f_y_recv(2, j // 2)
+
+        value = lax.dot_general(
+            hidden[...].reshape(4 * rows, units), wd[p], (((1,), (1,)), ((), ())),
+            preferred_element_type=F32,
+        )
+        value = value.astype(BF16).reshape(4, rows, value.shape[1])
+        for g in range(4):
+            part[g, p] = value[g]
+        d_copy(0, p).start()
+        d_copy(1, p).start()
+
+        @pl.when(j >= 1)
+        def _():
+            d_sum(j - 1)
+
+        @pl.when(j >= 2)
+        def _():
+            d_done(j - 2)
+
+        return carry
+
+    lax.fori_loop(0, 8, down, 0)
+    d_sum(7)
+    d_done(6)
+    d_done(7)
+
+    o_core.wait_send()
+    o_y().wait_send()
+    for group in firsts:
+        for copy in group:
+            copy.wait_send()
+    for k in range(4):
+        z_wait_send(o_z(k))
+        o_x(k).wait_send()
+        o_c(k).wait_send()
+        for m in range(3):
+            z_wait_send(f_z(m, k))
+            f_y(m, k).wait_send()
+    n_copy(quarter, 0, at_x).wait_send()
+    n_copy(quarter, 1, at_core).wait_send()
+    n_copy(q_x, 2, at_core).wait_send()
+
+    def drain(p, carry):
+        for i in range(3):
+            d_copy(i, p).wait_send()
+        return carry
+
+    lax.fori_loop(0, 8, drain, 0)
+
+
+def per_device_kernel(
+    queries, new_kv, cache_pool, page_table, assignment, lengths, lambda_vectors, subln_gain,
+    residual, out_weight, norm_gain, gate_weight, up_weight, down_weight_t,
+):
+    rows, heads, wide = queries.shape
+    pages, page_len = cache_pool.shape[:2]
+    width, units = residual.shape[1], gate_weight.shape[1] // 4
+    cached = lengths[assignment[0]]
+    logical = jnp.argmax(
+        page_table[0][None, :] == jnp.arange(pages, dtype=jnp.int32)[:, None], axis=1
+    ).astype(jnp.int32)
+    position = logical[:, None] * page_len + jnp.arange(page_len, dtype=jnp.int32)[None, :]
+    bias = jnp.where(position < cached, 0.0, NEG_FILL).astype(F32).reshape(1, pages * page_len)
+    lam = (
+        jnp.exp(jnp.sum(lambda_vectors[0] * lambda_vectors[1]))
+        - jnp.exp(jnp.sum(lambda_vectors[2] * lambda_vectors[3]))
+        + LAMBDA_BASE
+    ).reshape(1)
+    kv = jnp.concatenate([cache_pool.reshape(pages * page_len, heads, 2 * wide), new_kv], axis=0)
+    kv = jnp.swapaxes(kv, 0, 1)
+    keys = kv.shape[1]
+    anyspace = pl.BlockSpec(memory_space=pl.ANY)
+    vmem = pl.BlockSpec(memory_space=pltpu.VMEM)
+    dma = pltpu.SemaphoreType.DMA
+    return pl.pallas_call(
+        layer_kernel,
+        out_shape=jax.ShapeDtypeStruct((rows, width), BF16),
+        in_specs=[pl.BlockSpec(memory_space=pltpu.SMEM)] + [vmem] * 4 + [anyspace] * 6,
+        out_specs=vmem,
+        scratch_shapes=[
+            pltpu.VMEM((heads, rows, wide), BF16),
+            pltpu.VMEM((heads, keys, 2 * wide), BF16),
+            pltpu.VMEM((rows, width), BF16),
+            pltpu.VMEM((4, 2, 256, width), BF16),
+            pltpu.VMEM((8, 256, units), BF16),
+            pltpu.VMEM((8, 256, units), BF16),
+            pltpu.VMEM((8, 256, units), BF16),
+            pltpu.VMEM((4, rows, width), BF16),
+            pltpu.VMEM((rows, width), BF16),
+            pltpu.VMEM((4, rows, units), BF16),
+            pltpu.VMEM((4, 8, rows, 256), BF16),
+            pltpu.VMEM((2, 8, rows, 256), BF16),
+            pltpu.VMEM((8, rows, 256), BF16),
+            pltpu.VMEM((8, rows, 256), BF16),
+            dma((2, heads)), dma((4,)), dma((3, 3)), dma((3, 3)), dma((3, 10)), dma((3, 10)),
+            dma((16,)), dma((16,)), dma((3,)), dma((3,)), dma((3, 8)), dma((3, 8)),
+        ],
+        compiler_params=pltpu.CompilerParams(
+            collective_id=0, has_side_effects=True, vmem_limit_bytes=62 * 2**20
+        ),
+        name="layer",
+    )(
+        lam, bias, subln_gain.reshape(1, -1), norm_gain.reshape(1, -1), residual,
+        jnp.swapaxes(queries, 0, 1), kv, out_weight, gate_weight, up_weight, down_weight_t,
+    )
+
+
 def solution(mesh):
     in_specs = (
         P("req", "mlp", None),
@@ -182,6 +685,7 @@
         P("req", "mlp"),
     )
     out_specs = P("req", "mlp")
+    small = mesh.shape["req"] == 32 and mesh.shape["mlp"] == 1
     return jax.shard_map(
-        per_device, mesh=mesh, in_specs=in_specs, out_specs=out_specs, check_vma=False
-    )
+        per_device_kernel if small else per_device, mesh=mesh, in_specs=in_specs, out_specs=out_specs, check_vma=False
+    )

time: 403 us -> 197 us (0.49)
  waiting for transfers between devices: 315 us -> 0 us
  Pallas kernels: 0 us -> 171 us
  matrix products: 48.9 us -> 0 us
  between operations: 15.9 us -> 2.11 us
  loops' own time: 4.33 us -> 0 us
    all_gather x4 -> x0, waiting for transfers between devices: 312 us -> none  [the longest x1 97 us: per_device(): lax.all_gather(up_weight, 'req', axis=0, tiled=True)]
    pallas_call x0 -> x1, Pallas kernels: none -> 171 us  [per_device_kernel(): pl.pallas_call(layer_kernel, out_shape=jax.ShapeDtypeStruct((rows, width)...]
    dot_general x15 -> x0, matrix products: 48.9 us -> none  [the longest x1 13.8 us: per_device(): lax.dot_general(hidden_act, lax.all_gather(down_weight_t, 'req', axis=0,...]
    unnamed x23 -> x9, local copies, waits for them, and re-layouts: 2.04 us -> 12.6 us
    transpose x0 -> x1, other arithmetic: none -> 6.74 us  [per_device_kernel(): kv = jnp.swapaxes(kv, 0, 1)]
    another operation x1 -> x0, loops' own time: 4.33 us -> none  [attend(): lax.fori_loop(jnp.int32(0), page_count, page_step, (fresh_state(), fresh_...]
  transfers between devices with their start and end apart: 4 -> 0, of which waited for: 4 -> 0; matrix products, arithmetic and copies ran while one was open for 13% -> 0% of each run, Pallas kernels for 0% -> 0%
where the time goes in v1:
time: 197 us
  Pallas kernels  171 us (87%)
  local copies, waits for them, and re-layouts  13.9 us (7%)
  other arithmetic  10.3 us (5%)
  between operations  2.11 us (1%)
    pallas_call x1, Pallas kernels, per_device_kernel(): pl.pallas_call(layer_kernel, out_shape=jax.ShapeDtypeStruct((rows, width)...  171 us
    unnamed x9, local copies, waits for them, and re-layouts  12.6 us
    transpose x1, other arithmetic, per_device_kernel(): kv = jnp.swapaxes(kv, 0, 1)  6.74 us

profile of v1, /device:TPU:0, one launch (start us, length us, event | category | flops | bytes accessed | tf_op | source)
XLA Modules:
  0.0 197.2 jit_solution(8761955655440095063)
XLA Ops:
  0.7 1.2 dynamic_slice.3
  1.9 1.4 iota_reduce_fusion
  3.3 0.7 select_bitcast_fusion
  4.0 0.6 copy.25
  4.6 1.5 multiply_reduce_fusion
  7.5 0.0 copy-start
  7.5 7.9 %copy.19 = bf16[6,128,8,512]{3,1,0,2:T(8,128)(2,1)} copy(bf16[6,128,8,512]{3,2,1,0:T(8,128)(2,1)} %param.16) | data formatting | bytes 12582912 | tf_op args[2]
  15.4 0.0 copy-done
  15.4 0.7 copy.20
  16.1 0.0 copy-start.1
  16.1 6.7 %maximum_bitcast_fusion.kv_hbm = bf16[8,1024,512]{2,1,0:T(8,128)(2,1)} fusion(bf16[256,8,512]{2,0,1:T(8,128)(2,1)S(1)} %copy.20, bf16[768,8,512]{2,0,1:T(8,128)(2,1)} %bitcast.21), kind=kLoop, calls=%fused_computation | loop fusion | flops 16777216 | bytes 16777216 | tf_op jit(solution)/shard_map/transpose | solution.py:632
  22.8 0.0 copy-done.1
  22.8 1.2 copy.24
  24.0 170.9 %layer.1 = bf16[256,2048]{1,0:T(8,128)(2,1)} custom-call(f32[1]{0:T(128)} %bitcast.scale_ref, f32[1,768]{1,0:T(1,128)} %bitcast.23, f32[1,256]{1,0:T(1,128)} %bitcast.25, f32[1,2048]{1,0:T(1,128)} %bitcast.24, bf16[256,2048]{1,0:T(8,128)(2,1)} %residual_ref.1, bf16[8,256,256]{2,1,0:T(8,128)(2,1)} %bitcast.22, ...), custom_call_target="tpu_custom_call" | custom-call | tf_op jit(solution)/shard_map/layer/pallas_call | solution.py:637
  194.9 2.3 %copy.28 = bf16[256,2048]{1,0:T(8,128)(2,1)} copy(bf16[256,2048]{1,0:T(8,128)(2,1)} %layer.1) | data formatting | bytes 2097152
  (1 shorter events, 0.0 us)
Async XLA Ops:
  7.5 7.9 %copy-start = (bf16[256,8,512]{2,1,0:T(8,128)(2,1)S(1)}, bf16[256,8,512]{2,1,0:T(8,128)(2,1)}, u32[]{:S(2)}) copy-start(bf16[256,8,512]{2,1,0:T(8,128)(2,1)} %param.15) | copy-start | bytes 6291460
  16.1 6.8 %copy-start.1 = (bf16[256,8,256]{2,1,0:T(8,128)(2,1)S(1)}, bf16[256,8,256]{2,1,0:T(8,128)(2,1)}, u32[]{:S(2)}) copy-start(bf16[256,8,256]{2,1,0:T(8,128)(2,1)} %param.14) | copy-start | bytes 3145732

commit v2 on v1

--- a/solution.py
+++ b/solution.py
@@ -171,10 +171,10 @@
 
 
 def layer_kernel(
-    scale_ref, bias_ref, gain_ref, norm_ref, residual_ref,
-    q_hbm, kv_hbm, out_hbm, gate_hbm, up_hbm, down_hbm,
+    table_ref, request_ref, lengths_ref, lambda_ref, gain_ref, norm_ref, residual_ref,
+    q_hbm, kv_hbm, pool_hbm, out_hbm, gate_hbm, up_hbm, down_hbm,
     result_ref,
-    q_buf, kv_buf, attn, wo, wg, wu, wd, normed, stream, hidden, part, got_core, to_x, got_x,
+    q_raw, kv_raw, q_buf, kv_buf, attn, wo, wg, wu, wd, normed, stream, hidden, part, got_core, to_x, got_x,
     load_sem, own_sem, first_send, first_recv, far_send, far_recv, o_send, o_recv,
     n_send, n_recv, d_send, d_recv,
 ):
@@ -270,18 +270,21 @@
             group.append(copy)
         firsts.append(group)
 
-    def load(h):
-        return (
-            pltpu.make_async_copy(q_hbm.at[h], q_buf.at[h], load_sem.at[0, h]),
-            pltpu.make_async_copy(kv_hbm.at[h], kv_buf.at[h], load_sem.at[1, h]),
-        )
-
-    def start_load(h, carry):
-        for copy in load(h):
-            copy.start()
-        return carry
-
-    lax.fori_loop(0, heads, start_load, 0)
+    pages, page_len = pool_hbm.shape[:2]
+    chunks = pages + rows // page_len
+
+    q_load = pltpu.make_async_copy(q_hbm, q_raw, load_sem.at[chunks])
+    q_load.start()
+
+    def chunk_load(i):
+        if i < pages:
+            src = pool_hbm.at[i]
+        else:
+            src = kv_hbm.at[pl.ds((i - pages) * page_len, page_len)]
+        return pltpu.make_async_copy(src, kv_raw.at[i], load_sem.at[i])
+
+    for i in range(chunks):
+        chunk_load(i).start()
 
     mats = (wg, wu, wd)
 
@@ -409,23 +412,68 @@
     def z_open(m):
         z_start(f_z(m, 0))
 
+    def split(at_mid, at_end):
+        @pl.when(is_mid)
+        def _():
+            at_mid()
+
+        @pl.when(is_end)
+        def _():
+            at_end()
+
+    def run_events(step, at_mid, at_end):
+        for place_at, events in ((is_mid, at_mid), (is_end, at_end)):
+            for i, event in events.items():
+                @pl.when(jnp.logical_and(place_at, step == i))
+                def _(event=event):
+                    event()
+
     o_first()
-    f_first(0)
-    o_second()
-
-    events = {
-        0: lambda: f_first(1),
-        1: lambda: (z_open(0), o_pass(1), o_share(0)),
-        2: lambda: f_first(2),
-        3: lambda: (o_pass(2), z_open(1)),
-        4: lambda: (o_share(1), f_pass(0, 1)),
-        5: lambda: (o_pass(3), o_share(2)),
-        6: lambda: (f_pass(0, 2), z_open(2)),
-        7: lambda: (f_pass(1, 1), f_pass(0, 3)),
+
+    q_load.wait()
+    for i in range(rows // page_len):
+        span = pl.ds(i * page_len, page_len)
+        q_buf[:, span, :] = jnp.swapaxes(q_raw[span], 0, 1)
+
+    chunk_events = {1: o_second, 3: lambda: f_first(0), 5: lambda: f_first(1), 7: lambda: f_first(2)}
+
+    def turn(i, carry):
+        pltpu.make_async_copy(pool_hbm.at[0], kv_raw.at[i], load_sem.at[i]).wait()
+        span = pl.ds(pl.multiple_of(i * page_len, page_len), page_len)
+        kv_buf[:, span, :] = jnp.swapaxes(kv_raw[i], 0, 1)
+        run_events(i, chunk_events, chunk_events)
+        return carry
+
+    lax.fori_loop(0, chunks, turn, 0)
+
+    mid_events = {
+        3: lambda: (o_pass(2), o_pass(1), o_share(0), z_open(0)),
+        6: lambda: (o_share(1), o_pass(3)),
+        7: lambda: (f_pass(0, 1), z_open(1), o_share(2)),
     }
-
-    lam = scale_ref[0]
-    bias = bias_ref[...]
+    end_events = {
+        2: lambda: z_open(0),
+        3: lambda: (o_pass(1), o_share(0)),
+        4: lambda: z_open(1),
+        6: lambda: (o_share(1), z_open(2)),
+        7: lambda: o_pass(2),
+    }
+
+    vectors = lambda_ref[...]
+    lam = (
+        jnp.exp(jnp.sum(vectors[0:1] * vectors[1:2], axis=1, keepdims=True))
+        - jnp.exp(jnp.sum(vectors[2:3] * vectors[3:4], axis=1, keepdims=True))
+        + LAMBDA_BASE
+    )
+    length = lengths_ref[request_ref[0]]
+    within = lax.broadcasted_iota(jnp.int32, (1, page_len), 1)
+    pieces = []
+    for page in range(pages):
+        logical = jnp.int32(0)
+        for j in range(pages):
+            logical = logical + jnp.where(table_ref[0, j] == page, j, 0)
+        pieces.append(jnp.where(within + logical * page_len < length, 0.0, NEG_FILL))
+    bias = jnp.concatenate(pieces, axis=1).astype(F32)
     causal = jnp.where(
         lax.broadcasted_iota(jnp.int32, (rows, rows), 1)
         <= lax.broadcasted_iota(jnp.int32, (rows, rows), 0),
@@ -434,8 +482,6 @@
     ).astype(F32)
 
     def head_step(h, carry):
-        for copy in load(h):
-            copy.wait()
         values = kv_buf[h, :, wide:]
         mixed = []
         for one in range(2):
@@ -455,17 +501,15 @@
         mix = mix * lax.rsqrt(jnp.mean(mix * mix, axis=1, keepdims=True) + 1e-05)
         mix = mix * gain_ref[...] * (1.0 - LAMBDA_BASE)
         attn[:, pl.ds(pl.multiple_of(h * wide, 128), wide)] = mix.astype(BF16)
-        for i, event in events.items():
-            @pl.when(h == i)
-            def _(event=event):
-                event()
+        run_events(h, mid_events, end_events)
         return carry
 
     lax.fori_loop(0, heads, head_step, 0)
 
-    o_share(3)
-    f_pass(1, 2)
-    f_pass(1, 3)
+    split(
+        lambda: (f_pass(0, 2), o_share(3), f_pass(0, 3)),
+        lambda: (o_share(2), o_pass(3), f_pass(0, 1), o_share(3)),
+    )
     for k in range(4):
         o_shared(k)
 
@@ -489,22 +533,31 @@
 
     n_copy(quarter, 0, at_x).start()
     n_copy(quarter, 1, at_core).start()
-    f_pass(2, 1)
+    def relay():
+        n_copy(q_x, 0, at_x).wait_recv()
+        n_copy(q_x, 2, at_core).start()
+
+    split(
+        lambda: (
+            f_pass(1, 1), f_pass(1, 2), f_pass(1, 3), z_open(2), relay(),
+            f_pass(2, 1), f_pass(2, 2), f_pass(2, 3),
+        ),
+        lambda: (
+            f_pass(0, 2), f_pass(0, 3), f_pass(1, 1), relay(), f_pass(1, 2), f_pass(1, 3),
+        ),
+    )
     for m in range(2):
         for k in range(4):
             f_y_recv(m, k)
 
+    feed_events = {1: lambda: f_pass(2, 1), 3: lambda: f_pass(2, 2)}
+
     def feed(i, carry):
+        run_events(i, {}, feed_events)
+
         @pl.when(i == 1)
         def _():
             n_copy(q_core, 1, at_core).wait_recv()
-            f_pass(2, 2)
-
-        @pl.when(i == 2)
-        def _():
-            n_copy(q_x, 0, at_x).wait_recv()
-            n_copy(q_x, 2, at_core).start()
-            f_pass(2, 3)
 
         @pl.when(i == 3)
         def _():
@@ -570,6 +623,8 @@
             part[g, p] = value[g]
         d_copy(0, p).start()
         d_copy(1, p).start()
+
+        run_events(j, {}, {5: lambda: f_pass(2, 3)})
 
         @pl.when(j >= 1)
         def _():
@@ -617,29 +672,18 @@
     rows, heads, wide = queries.shape
     pages, page_len = cache_pool.shape[:2]
     width, units = residual.shape[1], gate_weight.shape[1] // 4
-    cached = lengths[assignment[0]]
-    logical = jnp.argmax(
-        page_table[0][None, :] == jnp.arange(pages, dtype=jnp.int32)[:, None], axis=1
-    ).astype(jnp.int32)
-    position = logical[:, None] * page_len + jnp.arange(page_len, dtype=jnp.int32)[None, :]
-    bias = jnp.where(position < cached, 0.0, NEG_FILL).astype(F32).reshape(1, pages * page_len)
-    lam = (
-        jnp.exp(jnp.sum(lambda_vectors[0] * lambda_vectors[1]))
-        - jnp.exp(jnp.sum(lambda_vectors[2] * lambda_vectors[3]))
-        + LAMBDA_BASE
-    ).reshape(1)
-    kv = jnp.concatenate([cache_pool.reshape(pages * page_len, heads, 2 * wide), new_kv], axis=0)
-    kv = jnp.swapaxes(kv, 0, 1)
-    keys = kv.shape[1]
+    keys = pages * page_len + rows
     anyspace = pl.BlockSpec(memory_space=pl.ANY)
     vmem = pl.BlockSpec(memory_space=pltpu.VMEM)
     dma = pltpu.SemaphoreType.DMA
     return pl.pallas_call(
         layer_kernel,
         out_shape=jax.ShapeDtypeStruct((rows, width), BF16),
-        in_specs=[pl.BlockSpec(memory_space=pltpu.SMEM)] + [vmem] * 4 + [anyspace] * 6,
+        in_specs=[pl.BlockSpec(memory_space=pltpu.SMEM)] * 3 + [vmem] * 4 + [anyspace] * 7,
         out_specs=vmem,
         scratch_shapes=[
+            pltpu.VMEM((rows, heads, wide), BF16),
+            pltpu.VMEM((keys // page_len, page_len, heads, 2 * wide), BF16),
             pltpu.VMEM((heads, rows, wide), BF16),
             pltpu.VMEM((heads, keys, 2 * wide), BF16),
             pltpu.VMEM((rows, width), BF16),
@@ -654,7 +698,7 @@
             pltpu.VMEM((2, 8, rows, 256), BF16),
             pltpu.VMEM((8, rows, 256), BF16),
             pltpu.VMEM((8, rows, 256), BF16),
-            dma((2, heads)), dma((4,)), dma((3, 3)), dma((3, 3)), dma((3, 10)), dma((3, 10)),
+            dma((keys // page_len + 1,)), dma((4,)), dma((3, 3)), dma((3, 3)), dma((3, 10)), dma((3, 10)),
             dma((16,)), dma((16,)), dma((3,)), dma((3,)), dma((3, 8)), dma((3, 8)),
         ],
         compiler_params=pltpu.CompilerParams(
@@ -662,8 +706,9 @@
         ),
         name="layer",
     )(
-        lam, bias, subln_gain.reshape(1, -1), norm_gain.reshape(1, -1), residual,
-        jnp.swapaxes(queries, 0, 1), kv, out_weight, gate_weight, up_weight, down_weight_t,
+        page_table, assignment, lengths, lambda_vectors, subln_gain.reshape(1, -1),
+        norm_gain.reshape(1, -1), residual, queries, new_kv, cache_pool,
+        out_weight, gate_weight, up_weight, down_weight_t,
     )
 
 

time: 197 us -> 174 us (0.88)
  local copies, waits for them, and re-layouts: 13.9 us -> 2.3 us
  other arithmetic: 10.3 us -> 0 us
    unnamed x9 -> x1, local copies, waits for them, and re-layouts: 12.6 us -> 2.3 us
    transpose x1 -> x0, other arithmetic: 6.74 us -> none  [per_device_kernel(): kv = jnp.swapaxes(kv, 0, 1)]
where the time goes in v2:
time: 174 us
  Pallas kernels  171 us (98%)
  local copies, waits for them, and re-layouts  2.3 us (1%)
    pallas_call x1, Pallas kernels, per_device_kernel(): pl.pallas_call(layer_kernel, out_shape=jax.ShapeDtypeStruct((rows, width)...  171 us

profile of v2, /device:TPU:0, one launch (start us, length us, event | category | flops | bytes accessed | tf_op | source)
XLA Modules:
  0.0 174.0 jit_solution(6203696872860541888)
XLA Ops:
  0.7 171.0 %layer.1 = bf16[256,2048]{1,0:T(8,128)(2,1)} custom-call(s32[1,6]{1,0:T(1,128)} %table_ref.1, s32[1]{0:T(128)S(6)} %copy.16.request_ref, s32[32]{0:T(128)} %lengths_ref.1, f32[4,128]{1,0:T(4,128)} %lambda_ref.1, f32[1,256]{1,0:T(1,128)} %bitcast.3, f32[1,2048]{1,0:T(1,128)} %bitcast.2, bf16[256,2048]{1,0:T(8,128)(2,1)} %residual_ref.1, ...), custom_call_target="tpu_custom_call" | custom-call | tf_op jit(solution)/shard_map/layer/pallas_call | solution.py:679
  171.7 2.3 %copy.17 = bf16[256,2048]{1,0:T(8,128)(2,1)} copy(bf16[256,2048]{1,0:T(8,128)(2,1)} %layer.1) | data formatting | bytes 2097152

commit v3 on v2

--- a/solution.py
+++ b/solution.py
@@ -175,7 +175,7 @@
     q_hbm, kv_hbm, pool_hbm, out_hbm, gate_hbm, up_hbm, down_hbm,
     result_ref,
     q_raw, kv_raw, q_buf, kv_buf, attn, wo, wg, wu, wd, normed, stream, hidden, part, got_core, to_x, got_x,
-    load_sem, own_sem, first_send, first_recv, far_send, far_recv, o_send, o_recv,
+    load_sem, own_sem, first_send, first_recv, far_send, far_recv, oz_send, oz_recv, o_send, o_recv,
     n_send, n_recv, d_send, d_recv,
 ):
     heads = q_buf.shape[0]
@@ -332,46 +332,56 @@
             for copy in for_mid:
                 copy.wait_send()
 
-    def f_block(m):
-        return lambda zz: mats[m].at[zz * 2 + y]
-
-    def f_z(m, k):
+    def f_block(m, part):
+        span = pl.ds(part * (mats[m].shape[1] // 2), mats[m].shape[1] // 2)
+        return lambda zz: mats[m].at[zz * 2 + y, span]
+
+    def f_z(m, k, part):
         return along_z(
-            f_block(m), lambda i: far_send.at[m, i], lambda i: far_recv.at[m, i], k
+            f_block(m, part),
+            lambda i: far_send.at[m, part, i],
+            lambda i: far_recv.at[m, part, i],
+            k,
         )
 
-    def f_z_recv(m, k):
-        block = f_block(m)(order(k))
-        send(block, block, far_send.at[m, k], far_recv.at[m, k], at_y).wait_recv()
-
-    def f_y(m, k):
-        block = f_block(m)(order(k))
-        return send(block, block, far_send.at[m, 6 + k], far_recv.at[m, 6 + k], at_y)
+    def f_z_recv(m, k, part):
+        block = f_block(m, part)(order(k))
+        send(block, block, far_send.at[m, part, k], far_recv.at[m, part, k], at_y).wait_recv()
+
+    def f_y(m, k, part):
+        block = f_block(m, part)(order(k))
+        return send(block, block, far_send.at[m, part, 6 + k], far_recv.at[m, part, 6 + k], at_y)
 
     def f_y_recv(m, k):
-        block = mats[m].at[order(k) * 2 + 1 - y]
-        send(block, block, far_send.at[m, 6 + k], far_recv.at[m, 6 + k], at_y).wait_recv()
+        for part in range(2):
+            half_rows = mats[m].shape[1] // 2
+            block = mats[m].at[order(k) * 2 + 1 - y, pl.ds(part * half_rows, half_rows)]
+            send(
+                block, block, far_send.at[m, part, 6 + k], far_recv.at[m, part, 6 + k], at_y
+            ).wait_recv()
 
     def f_first(m):
         owns[m].wait()
         for i, q_from in enumerate((q_core, q_x, q_diag)):
             block = mats[m].at[z * 2 + y, pl.ds(pl.multiple_of(q_from * shard, 64), shard)]
             send(block, block, first_send.at[m, i], first_recv.at[m, i], at_core).wait_recv()
-        f_y(m, 0).start()
+        for part in range(2):
+            f_y(m, 0, part).start()
 
     def f_pass(m, k):
-        f_z_recv(m, k)
-        z_start(f_z(m, k))
-        f_y(m, k).start()
-
-    def o_block(zz):
-        return wo.at[zz, :, x_rows, my_half]
-
-    def o_z(k):
-        return along_z(o_block, lambda i: o_send.at[1 + i], lambda i: o_recv.at[1 + i], k)
+        for part in range(2):
+            f_z_recv(m, k, part)
+            z_start(f_z(m, k, part))
+            f_y(m, k, part).start()
+
+    def o_block(s):
+        return lambda zz: wo.at[zz, (y + s) % 2, x_rows, my_half]
+
+    def o_z(k, s):
+        return along_z(o_block(s), lambda i: oz_send.at[s, i], lambda i: oz_recv.at[s, i], k)
 
     def o_x(k):
-        block = o_block(order(k))
+        block = wo.at[order(k), :, x_rows, my_half]
         return send(block, block, o_send.at[8 + k], o_recv.at[8 + k], at_x)
 
     def o_c(k):
@@ -386,18 +396,20 @@
         o_own.wait()
         block = wo.at[z, y, core_rows, my_half]
         send(block, block, o_send.at[0], o_recv.at[0], at_core).wait_recv()
+        z_start(o_z(0, 0))
         o_y().start()
 
     def o_second():
         block = wo.at[z, 1 - y, x_rows, my_half]
         send(block, block, o_send.at[1], o_recv.at[1], at_y).wait_recv()
-        z_start(o_z(0))
+        z_start(o_z(0, 1))
         o_x(0).start()
 
     def o_pass(k):
-        block = o_block(order(k))
-        send(block, block, o_send.at[1 + k], o_recv.at[1 + k], at_y).wait_recv()
-        z_start(o_z(k))
+        for s in range(2):
+            block = o_block(s)(order(k))
+            send(block, block, oz_send.at[s, k], oz_recv.at[s, k], at_y).wait_recv()
+            z_start(o_z(k, s))
         o_x(k).start()
 
     def o_share(k):
@@ -410,7 +422,8 @@
         send(block, block, o_send.at[12 + k], o_recv.at[12 + k], at_core).wait_recv()
 
     def z_open(m):
-        z_start(f_z(m, 0))
+        for part in range(2):
+            z_start(f_z(m, 0, part))
 
     def split(at_mid, at_end):
         @pl.when(is_mid)
@@ -447,9 +460,11 @@
     lax.fori_loop(0, chunks, turn, 0)
 
     mid_events = {
-        3: lambda: (o_pass(2), o_pass(1), o_share(0), z_open(0)),
-        6: lambda: (o_share(1), o_pass(3)),
-        7: lambda: (f_pass(0, 1), z_open(1), o_share(2)),
+        2: lambda: z_open(0),
+        3: lambda: (o_pass(2), o_pass(1), o_share(0)),
+        5: lambda: (o_share(1), z_open(1)),
+        6: lambda: o_pass(3),
+        7: lambda: (f_pass(0, 1), o_share(2)),
     }
     end_events = {
         2: lambda: z_open(0),
@@ -550,7 +565,7 @@
         for k in range(4):
             f_y_recv(m, k)
 
-    feed_events = {1: lambda: f_pass(2, 1), 3: lambda: f_pass(2, 2)}
+    feed_events = {1: lambda: f_pass(2, 1)}
 
     def feed(i, carry):
         run_events(i, {}, feed_events)
@@ -624,8 +639,6 @@
         d_copy(0, p).start()
         d_copy(1, p).start()
 
-        run_events(j, {}, {5: lambda: f_pass(2, 3)})
-
         @pl.when(j >= 1)
         def _():
             d_sum(j - 1)
@@ -634,6 +647,7 @@
         def _():
             d_done(j - 2)
 
+        run_events(j, {}, {2: lambda: f_pass(2, 2), 4: lambda: f_pass(2, 3)})
         return carry
 
     lax.fori_loop(0, 8, down, 0)
@@ -647,12 +661,14 @@
         for copy in group:
             copy.wait_send()
     for k in range(4):
-        z_wait_send(o_z(k))
+        for s in range(2):
+            z_wait_send(o_z(k, s))
         o_x(k).wait_send()
         o_c(k).wait_send()
         for m in range(3):
-            z_wait_send(f_z(m, k))
-            f_y(m, k).wait_send()
+            for cut in range(2):
+                z_wait_send(f_z(m, k, cut))
+                f_y(m, k, cut).wait_send()
     n_copy(quarter, 0, at_x).wait_send()
     n_copy(quarter, 1, at_core).wait_send()
     n_copy(q_x, 2, at_core).wait_send()
@@ -698,7 +714,8 @@
             pltpu.VMEM((2, 8, rows, 256), BF16),
             pltpu.VMEM((8, rows, 256), BF16),
             pltpu.VMEM((8, rows, 256), BF16),
-            dma((keys // page_len + 1,)), dma((4,)), dma((3, 3)), dma((3, 3)), dma((3, 10)), dma((3, 10)),
+            dma((keys // page_len + 1,)), dma((4,)), dma((3, 3)), dma((3, 3)), dma((3, 2, 10)), dma((3, 2, 10)),
+            dma((2, 6)), dma((2, 6)),
             dma((16,)), dma((16,)), dma((3,)), dma((3,)), dma((3, 8)), dma((3, 8)),
         ],
         compiler_params=pltpu.CompilerParams(

time: 174 us -> 182 us (1.046)
  Pallas kernels: 171 us -> 179 us
    pallas_call x1, Pallas kernels: 171 us -> 179 us  [per_device_kernel(): pl.pallas_call(layer_kernel, out_shape=jax.ShapeDtypeStruct((rows, width)...]
where the time goes in v3:
time: 182 us
  Pallas kernels  179 us (98%)
  local copies, waits for them, and re-layouts  2.3 us (1%)
    pallas_call x1, Pallas kernels, per_device_kernel(): pl.pallas_call(layer_kernel, out_shape=jax.ShapeDtypeStruct((rows, width)...  179 us

profile of v3, /device:TPU:0, one launch (start us, length us, event | category | flops | bytes accessed | tf_op | source)
XLA Modules:
  0.0 182.2 jit_solution(14727837218964895781)
XLA Ops:
  0.7 179.2 %layer.1 = bf16[256,2048]{1,0:T(8,128)(2,1)} custom-call(s32[1,6]{1,0:T(1,128)} %table_ref.1, s32[1]{0:T(128)S(6)} %copy.16.request_ref, s32[32]{0:T(128)} %lengths_ref.1, f32[4,128]{1,0:T(4,128)} %lambda_ref.1, f32[1,256]{1,0:T(1,128)} %bitcast.3, f32[1,2048]{1,0:T(1,128)} %bitcast.2, bf16[256,2048]{1,0:T(8,128)(2,1)} %residual_ref.1, ...), custom_call_target="tpu_custom_call" | custom-call | tf_op jit(solution)/shard_map/layer/pallas_call | solution.py:695
  179.9 2.3 %copy.17 = bf16[256,2048]{1,0:T(8,128)(2,1)} copy(bf16[256,2048]{1,0:T(8,128)(2,1)} %layer.1) | data formatting | bytes 2097152

commit v4 on v3

--- a/solution.py
+++ b/solution.py
@@ -460,11 +460,11 @@
     lax.fori_loop(0, chunks, turn, 0)
 
     mid_events = {
-        2: lambda: z_open(0),
-        3: lambda: (o_pass(2), o_pass(1), o_share(0)),
-        5: lambda: (o_share(1), z_open(1)),
-        6: lambda: o_pass(3),
-        7: lambda: (f_pass(0, 1), o_share(2)),
+        2: lambda: (o_pass(2), o_pass(1)),
+        3: lambda: (o_share(0), z_open(0)),
+        5: lambda: o_pass(3),
+        6: lambda: (o_share(1), z_open(1), f_pass(0, 1)),
+        7: lambda: (f_pass(0, 2), f_pass(1, 1)),
     }
     end_events = {
         2: lambda: z_open(0),
@@ -522,8 +522,14 @@
     lax.fori_loop(0, heads, head_step, 0)
 
     split(
-        lambda: (f_pass(0, 2), o_share(3), f_pass(0, 3)),
-        lambda: (o_share(2), o_pass(3), f_pass(0, 1), o_share(3)),
+        lambda: (
+            o_share(2), f_pass(0, 3), f_pass(1, 2), f_pass(1, 3), o_share(3), z_open(2),
+            f_pass(2, 1), f_pass(2, 2),
+        ),
+        lambda: (
+            f_pass(0, 1), o_share(2), o_pass(3), f_pass(1, 1), f_pass(0, 2), o_share(3),
+            f_pass(0, 3),
+        ),
     )
     for k in range(4):
         o_shared(k)
@@ -553,19 +559,14 @@
         n_copy(q_x, 2, at_core).start()
 
     split(
-        lambda: (
-            f_pass(1, 1), f_pass(1, 2), f_pass(1, 3), z_open(2), relay(),
-            f_pass(2, 1), f_pass(2, 2), f_pass(2, 3),
-        ),
-        lambda: (
-            f_pass(0, 2), f_pass(0, 3), f_pass(1, 1), relay(), f_pass(1, 2), f_pass(1, 3),
-        ),
+        lambda: f_pass(2, 3),
+        lambda: (f_pass(1, 2), f_pass(1, 3), f_pass(2, 1)),
     )
     for m in range(2):
         for k in range(4):
             f_y_recv(m, k)
 
-    feed_events = {1: lambda: f_pass(2, 1)}
+    feed_events = {1: lambda: f_pass(2, 2), 3: lambda: f_pass(2, 3)}
 
     def feed(i, carry):
         run_events(i, {}, feed_events)
@@ -573,6 +574,10 @@
         @pl.when(i == 1)
         def _():
             n_copy(q_core, 1, at_core).wait_recv()
+
+        @pl.when(i == 2)
+        def _():
+            relay()
 
         @pl.when(i == 3)
         def _():
@@ -647,7 +652,6 @@
         def _():
             d_done(j - 2)
 
-        run_events(j, {}, {2: lambda: f_pass(2, 2), 4: lambda: f_pass(2, 3)})
         return carry
 
     lax.fori_loop(0, 8, down, 0)

time: 182 us -> 159 us (0.87)
  Pallas kernels: 179 us -> 156 us
    pallas_call x1, Pallas kernels: 179 us -> 156 us  [per_device_kernel(): pl.pallas_call(layer_kernel, out_shape=jax.ShapeDtypeStruct((rows, width)...]
where the time goes in v4:
time: 159 us
  Pallas kernels  156 us (98%)
  local copies, waits for them, and re-layouts  2.3 us (1%)
    pallas_call x1, Pallas kernels, per_device_kernel(): pl.pallas_call(layer_kernel, out_shape=jax.ShapeDtypeStruct((rows, width)...  156 us

profile of v4, /device:TPU:0, one launch (start us, length us, event | category | flops | bytes accessed | tf_op | source)
XLA Modules:
  0.0 159.1 jit_solution(11006679917939821097)
XLA Ops:
  0.7 156.2 %layer.1 = bf16[256,2048]{1,0:T(8,128)(2,1)} custom-call(s32[1,6]{1,0:T(1,128)} %table_ref.1, s32[1]{0:T(128)S(6)} %copy.16.request_ref, s32[32]{0:T(128)} %lengths_ref.1, f32[4,128]{1,0:T(4,128)} %lambda_ref.1, f32[1,256]{1,0:T(1,128)} %bitcast.3, f32[1,2048]{1,0:T(1,128)} %bitcast.2, bf16[256,2048]{1,0:T(8,128)(2,1)} %residual_ref.1, ...), custom_call_target="tpu_custom_call" | custom-call | tf_op jit(solution)/shard_map/layer/pallas_call | solution.py:699
  156.8 2.3 %copy.17 = bf16[256,2048]{1,0:T(8,128)(2,1)} copy(bf16[256,2048]{1,0:T(8,128)(2,1)} %layer.1) | data formatting | bytes 2097152

commit v5 on v4

--- a/solution.py
+++ b/solution.py
@@ -448,30 +448,42 @@
         span = pl.ds(i * page_len, page_len)
         q_buf[:, span, :] = jnp.swapaxes(q_raw[span], 0, 1)
 
-    chunk_events = {1: o_second, 3: lambda: f_first(0), 5: lambda: f_first(1), 7: lambda: f_first(2)}
+    both_chunk = {
+        0: o_second, 1: lambda: f_first(0), 2: lambda: f_first(1), 3: lambda: f_first(2),
+        5: lambda: (o_share(0), z_open(0)),
+    }
+    mid_chunk = both_chunk | {
+        4: lambda: (o_pass(2), o_pass(1)), 7: lambda: (o_pass(3), z_open(1))
+    }
+    end_chunk = both_chunk | {6: lambda: (o_pass(1), z_open(1))}
 
     def turn(i, carry):
         pltpu.make_async_copy(pool_hbm.at[0], kv_raw.at[i], load_sem.at[i]).wait()
         span = pl.ds(pl.multiple_of(i * page_len, page_len), page_len)
         kv_buf[:, span, :] = jnp.swapaxes(kv_raw[i], 0, 1)
-        run_events(i, chunk_events, chunk_events)
+        run_events(i, mid_chunk, end_chunk)
         return carry
 
     lax.fori_loop(0, chunks, turn, 0)
 
     mid_events = {
-        2: lambda: (o_pass(2), o_pass(1)),
-        3: lambda: (o_share(0), z_open(0)),
-        5: lambda: o_pass(3),
-        6: lambda: (o_share(1), z_open(1), f_pass(0, 1)),
-        7: lambda: (f_pass(0, 2), f_pass(1, 1)),
+        0: lambda: o_share(1),
+        1: lambda: f_pass(0, 1),
+        2: lambda: f_pass(0, 2),
+        3: lambda: f_pass(1, 1),
+        4: lambda: (o_share(2), f_pass(0, 3)),
+        5: lambda: f_pass(1, 2),
+        6: lambda: (f_pass(1, 3), o_share(3)),
+        7: lambda: z_open(2),
     }
     end_events = {
-        2: lambda: z_open(0),
-        3: lambda: (o_pass(1), o_share(0)),
-        4: lambda: z_open(1),
-        6: lambda: (o_share(1), z_open(2)),
-        7: lambda: o_pass(2),
+        0: lambda: o_share(1),
+        1: lambda: (o_pass(2), z_open(2)),
+        2: lambda: f_pass(0, 1),
+        4: lambda: o_share(2),
+        5: lambda: o_pass(3),
+        6: lambda: (f_pass(1, 1), f_pass(0, 2)),
+        7: lambda: o_share(3),
     }
 
     vectors = lambda_ref[...]
@@ -522,14 +534,8 @@
     lax.fori_loop(0, heads, head_step, 0)
 
     split(
-        lambda: (
-            o_share(2), f_pass(0, 3), f_pass(1, 2), f_pass(1, 3), o_share(3), z_open(2),
-            f_pass(2, 1), f_pass(2, 2),
-        ),
-        lambda: (
-            f_pass(0, 1), o_share(2), o_pass(3), f_pass(1, 1), f_pass(0, 2), o_share(3),
-            f_pass(0, 3),
-        ),
+        lambda: (f_pass(2, 1), f_pass(2, 2)),
+        lambda: f_pass(0, 3),
     )
     for k in range(4):
         o_shared(k)

time: 159 us -> 156 us (0.981)
  Pallas kernels: 156 us -> 153 us
    pallas_call x1, Pallas kernels: 156 us -> 153 us  [per_device_kernel(): pl.pallas_call(layer_kernel, out_shape=jax.ShapeDtypeStruct((rows, width)...]
where the time goes in v5:
time: 156 us
  Pallas kernels  153 us (98%)
  local copies, waits for them, and re-layouts  2.3 us (1%)
    pallas_call x1, Pallas kernels, per_device_kernel(): pl.pallas_call(layer_kernel, out_shape=jax.ShapeDtypeStruct((rows, width)...  153 us

profile of v5, /device:TPU:0, one launch (start us, length us, event | category | flops | bytes accessed | tf_op | source)
XLA Modules:
  0.0 155.9 jit_solution(8278564451625277017)
XLA Ops:
  0.7 153.0 %layer.1 = bf16[256,2048]{1,0:T(8,128)(2,1)} custom-call(s32[1,6]{1,0:T(1,128)} %table_ref.1, s32[1]{0:T(128)S(6)} %copy.16.request_ref, s32[32]{0:T(128)} %lengths_ref.1, f32[4,128]{1,0:T(4,128)} %lambda_ref.1, f32[1,256]{1,0:T(1,128)} %bitcast.3, f32[1,2048]{1,0:T(1,128)} %bitcast.2, bf16[256,2048]{1,0:T(8,128)(2,1)} %residual_ref.1, ...), custom_call_target="tpu_custom_call" | custom-call | tf_op jit(solution)/shard_map/layer/pallas_call | solution.py:705
  153.6 2.3 %copy.17 = bf16[256,2048]{1,0:T(8,128)(2,1)} copy(bf16[256,2048]{1,0:T(8,128)(2,1)} %layer.1) | data formatting | bytes 2097152
